TPU v7x, 32 devices: a whole 2x2x4 slice. The times are simulated.
32 devices in a mesh: groups: 2 (over y), loop: 4 (over z), enc: 2 (over x), rep: 2 (over core).
Axes of the slice: x: 2, y: 2, z: 4, core: 2. Of those that a mesh axis runs over, the one named last changes fastest.
Arguments:
- embeddings: bfloat16 [4096, 768], P(('groups', 'loop', 'rep'), 'enc'), parts along dimension 0, may hold values from -24 to 24
- head_weight: bfloat16 [768, 768], P('enc'), may hold values from -0.21875 to 0.21875
- gp_weights: float32 [4096], P('groups'), parts along dimension 0, may hold values from -24 to 24
- counts: int32 [8], P('groups'), parts along dimension 0, may hold values from 64 to 512, as said below
Outputs:
- embed_grad: bfloat16 [4096, 768], P(('groups', 'loop', 'rep'), 'enc'), parts along dimension 0
- head_grad: float32 [1536, 768], P(('groups', 'enc')), parts along dimension 0
There are 2 independent parts, one for each index of `groups`. A program takes and returns all parts, laid end to end along the dimension named above; an argument that names none is the same for every part. Nothing has to cross between parts.
Inputs may be any that keep to these rules, and one draw needn't show every extreme that they name: `counts`: some block is full and some block holds exactly 64 valid molecules.
All inputs are finite; a program needn't handle non-finite values.
Results may differ from a plain program's by a relative error of at most 0.019.
Values may be sent and summed in bfloat16 or wider, within the bound.
A program may use at most 64 MiB of HBM per device.

v0:
```python
import jax
import jax.numpy as jnp
from jax import lax
from jax.sharding import PartitionSpec as P

EPSILON = 1e-06


def passed_along(value, axis, steps):
    count = lax.axis_size(axis)
    pairs = [(source, (source + steps) % count) for source in range(count)]
    return lax.ppermute(value, axis, pairs)


def pass_forward(piece):
    return passed_along(piece, "loop", 1)


def body(embeddings, head_weight, gp_weights, counts):
    enc_size = lax.axis_size("enc")
    rep_size = lax.axis_size("rep")
    loop_size = lax.axis_size("loop")
    share_rows = embeddings.shape[0]
    piece_rows = share_rows // enc_size
    block_rows = share_rows * rep_size
    loop_index = lax.axis_index("loop")
    enc_index = lax.axis_index("enc")
    rep_index = lax.axis_index("rep")
    rows = embeddings
    own_feats = lax.psum_scatter(
        jnp.dot(rows, head_weight, preferred_element_type=jnp.float32),
        "enc",
        scatter_dimension=0,
        tiled=True,
    ).astype(jnp.bfloat16)
    block_feats = lax.all_gather(own_feats, ("enc", "rep"), axis=0, tiled=True)
    block_norms = jnp.sum(jnp.square(block_feats.astype(jnp.float32)), axis=1)
    offsets = (
        jnp.arange(rep_size, dtype=jnp.int32)[None, :, None] * share_rows
        + jnp.arange(enc_size, dtype=jnp.int32)[:, None, None] * piece_rows
        + jnp.arange(piece_rows, dtype=jnp.int32)[None, None, :]
    ).reshape(block_rows)
    own_base = lax.dynamic_slice_in_dim(gp_weights, loop_index * block_rows, block_rows)
    block_coef = (
        own_base.reshape(rep_size, enc_size, piece_rows).transpose(1, 0, 2).reshape(block_rows)
    )
    own_count = lax.dynamic_index_in_dim(counts, loop_index, keepdims=False)
    block_coef = jnp.where(offsets < own_count, block_coef, 0.0)
    piece_start = rep_index * share_rows + enc_index * piece_rows
    piece_offsets = piece_start + jnp.arange(piece_rows, dtype=jnp.int32)

    def tile(state, piece, anchor):
        anchor_count = lax.dynamic_index_in_dim(counts, anchor, keepdims=False)
        accum, quotient_sum = state
        piece_coef = lax.dynamic_slice_in_dim(
            gp_weights, anchor * block_rows + piece_start, piece_rows
        )
        piece_coef = jnp.where(piece_offsets < anchor_count, piece_coef, 0.0)
        piece_norms = jnp.sum(jnp.square(piece.astype(jnp.float32)), axis=1)
        scores = lax.dot_general(
            piece, block_feats, (((1,), (1,)), ((), ())), preferred_element_type=jnp.float32
        )
        denom = piece_norms[:, None] + block_norms[None, :] - scores + EPSILON
        inverse = 1.0 / (denom * denom)
        pair_coef = piece_coef[:, None] * block_coef[None, :]
        pair_weight = (pair_coef * (piece_norms[:, None] + block_norms[None, :]) * inverse).astype(
            jnp.bfloat16
        )
        quotient_sum = quotient_sum + jnp.sum(pair_coef * 2.0 * scores * inverse, axis=0)
        accum = accum + lax.dot_general(
            pair_weight, piece, (((0,), (0,)), ((), ())), preferred_element_type=jnp.float32
        )
        return (accum, quotient_sum)

    start_state = (
        jnp.zeros((block_rows, block_feats.shape[1]), jnp.float32),
        jnp.zeros((block_rows,), jnp.float32),
    )
    state = tile(start_state, own_feats, loop_index)

    def forward_step(step_index, carry):
        moving, inner = carry
        moving = pass_forward(moving)
        inner = tile(inner, moving, (loop_index - step_index - 1 + loop_size) % loop_size)
        return (moving, inner)

    moving, state = lax.fori_loop(0, loop_size - 1, forward_step, (own_feats, state))
    accum, quotient_sum = state
    grad_block = accum - block_feats.astype(jnp.float32) * quotient_sum[:, None]
    own_grad = lax.psum_scatter(
        grad_block.astype(jnp.bfloat16), ("enc", "rep"), scatter_dimension=0, tiled=True
    )
    piece = lax.all_gather(own_grad, "enc", axis=0, tiled=True)
    back = lax.dot_general(
        piece, head_weight, (((1,), (1,)), ((), ())), preferred_element_type=jnp.float32
    )
    embed_part = back
    rows = embeddings
    head_part = lax.dot_general(
        rows, piece, (((0,), (0,)), ((), ())), preferred_element_type=jnp.float32
    )
    embed_part, head_part = (embed_part, head_part)
    head_grad = lax.psum(head_part, ("loop", "rep"))
    return (embed_part.astype(jnp.bfloat16), head_grad)


def solution(mesh):
    placed = (P(("groups", "loop", "rep"), "enc"), P("enc", None), P("groups"), P("groups"))
    return jax.shard_map(
        body,
        mesh=mesh,
        in_specs=placed,
        out_specs=(P(("groups", "loop", "rep"), "enc"), P(("groups", "enc"), None)),
        check_vma=False,
    )
```

profile of v0, /device:TPU:0, one launch (start us, length us, event | category | flops | bytes accessed | tf_op | source)
XLA Modules:
  0.0 170.0 jit_solution(11172648524668776611)
XLA Ops:
  7.2 1.0 copy-done
  8.2 2.2 %fusion.40 = f32[256,768]{1,0:T(8,128)} fusion(bf16[256,384]{1,0:T(8,128)(2,1)} %param.6, bf16[384,768]{1,0:T(8,128)(2,1)S(1)} %copy-done), kind=kOutput, calls=%fused_computation.56 | convolution fusion | flops 150994944 | bytes 1572864 | tf_op jit(solution)/shard_map/dot_general | solution.py:31
  10.5 0.7 dynamic_slice.37
  11.2 0.8 dynamic_slice.39
  12.0 0.8 compare_select_fusion.1
  12.8 1.5 compare_select_fusion.2
  14.2 16.8 %reduce-scatter.3.cloned.1.call-done = f32[128,768]{1,0:T(8,128)} async-done(((f32[256,768]{1,0:T(8,128)}), f32[128,768]{1,0:T(8,128)}) %reduce-scatter.3.cloned.1.call-update) | async-done | bytes 393232 | tf_op jit(solution)/shard_map/reduce_scatter | solution.py:30
  31.0 1.1 multiply_reduce_fusion.1
  32.1 8.2 %all_gather.6 = bf16[512,768]{1,0:T(8,128)(2,1)S(1)} all-gather(bf16[128,768]{1,0:T(8,128)(2,1)S(1)} %get-tuple-element.541), channel_id=1, replica_groups=mesh['groups'=2,'loop'=4,'enc'=2,'rep'=2] {'enc','rep'}, dimensions={0}, use_global_device_ids=true | all-gather | bytes 983040 | tf_op jit(solution)/shard_map/all_gather | solution.py:36
  41.0 0.5 fusion.30
  41.5 28.3 %while.23 = (s32[]{:T(128)}, bf16[128,768]{1,0:T(8,128)(2,1)S(1)}, f32[512,768]{1,0:T(8,128)S(1)}, f32[512]{0:T(512)S(1)}, s32[]{:T(128)}, /*index=5*/s32[4]{0:T...) while((s32[]{:T(128)}, bf16[128,768]{1,0:T(8,128)(2,1)S(1)}, ...), condition=%wide.region_7.8_spmd.clone.clone, body=%wide.region_4.7_spmd.clone.clone.sunk | while | flops 203260192 | bytes 6246334 | solution.py:87
  41.5 1.5 collective-permute-start
  43.1 0.6 dynamic_slice.49
  43.6 1.4 compare_select_fusion.4
  45.1 5.5 %collective-permute-done = bf16[128,768]{1,0:T(8,128)(2,1)S(1)} collective-permute-done((bf16[128,768]{1,0:T(8,128)(2,1)S(1)}, bf16[128,768]{1,0:T(8,128)(2,1)S(1)}, u32[]{:S(2)}, u32[]{:S(2)}) %collective-permute-start) | collective-permute-done | bytes 196640 | tf_op jit(solution)/shard_map/while/body/eval_jaxpr/ppermute | solution.py:12
  50.6 0.4 fusion.62
  51.1 0.6 convolution_add_fusion.2
  51.8 0.6 dynamic_slice.49
  52.4 1.4 compare_select_fusion.4
  53.8 6.1 %collective-permute-done = bf16[128,768]{1,0:T(8,128)(2,1)S(1)} collective-permute-done((bf16[128,768]{1,0:T(8,128)(2,1)S(1)}, bf16[128,768]{1,0:T(8,128)(2,1)S(1)}, u32[]{:S(2)}, u32[]{:S(2)}) %collective-permute-start) | collective-permute-done | bytes 196640 | tf_op jit(solution)/shard_map/while/body/eval_jaxpr/ppermute | solution.py:12
  60.5 0.6 convolution_add_fusion.2
  61.2 0.6 dynamic_slice.49
  61.8 1.4 compare_select_fusion.4
  63.2 5.4 %collective-permute-done = bf16[128,768]{1,0:T(8,128)(2,1)S(1)} collective-permute-done((bf16[128,768]{1,0:T(8,128)(2,1)S(1)}, bf16[128,768]{1,0:T(8,128)(2,1)S(1)}, u32[]{:S(2)}, u32[]{:S(2)}) %collective-permute-start) | collective-permute-done | bytes 196640 | tf_op jit(solution)/shard_map/while/body/eval_jaxpr/ppermute | solution.py:12
  69.2 0.6 convolution_add_fusion.2
  69.8 1.1 fusion.21
  71.1 20.9 %reduce-scatter.5.cloned.1.call-done = bf16[128,768]{1,0:T(8,128)(2,1)} async-done(((bf16[512,768]{1,0:T(8,128)(2,1)}), bf16[128,768]{1,0:T(8,128)(2,1)}) %reduce-scatter.5.cloned.1.call-update) | async-done | bytes 196624 | tf_op jit(solution)/shard_map/reduce_scatter | solution.py:90
  92.0 7.5 %all_gather.7 = bf16[256,768]{1,0:T(8,128)(2,1)S(1)} all-gather(bf16[128,768]{1,0:T(8,128)(2,1)} %reduce-scatter.5.cloned.1.call-done), channel_id=1, replica_groups=mesh['groups'=2,'loop'=4,'enc'=2,'rep'=2] {'enc'}, dimensions={0}, use_global_device_ids=true | all-gather | bytes 589824 | tf_op jit(solution)/shard_map/all_gather | solution.py:93
  99.5 1.4 convolution_bitcast_fusion
  100.9 1.1 convolution_convert_fusion
  102.0 58.8 %all-reduce.2.cloned.1.call-done = f32[384,768]{0,1:T(8,128)} async-done(((f32[384,768]{0,1:T(8,128)}), f32[384,768]{0,1:T(8,128)}) %all-reduce.2.cloned.1.call-update) | async-done | bytes 1179664 | tf_op jit(solution)/shard_map/psum | solution.py:103
  160.8 2.7 %copy.9 = f32[384,768]{1,0:T(8,128)} copy(f32[384,768]{0,1:T(8,128)} %all-reduce.2.cloned.1.call-done) | data formatting | bytes 2359296
  (29 shorter events, 2.4 us)
Async XLA Ops:
  7.2 1.1 copy-start
  7.2 3.3 %copy-start.2 = (s32[4]{0:T(128)S(1)}, s32[4]{0:T(128)}, u32[]{:S(2)}) copy-start(s32[4]{0:T(128)} %param.9) | copy-start | bytes 52
  7.2 23.8 %reduce-scatter.3.cloned.1.call-start = ((), (), s32[]{:S(2)}) async-start(), calls=%async_computation.2 | async-start | bytes 1179648 | tf_op jit(solution)/shard_map/reduce_scatter | solution.py:30
  10.4 81.6 %reduce-scatter.5.cloned.1.call-start = ((), (), s32[]{:S(2)}) async-start(), calls=%async_computation.3 | async-start | bytes 983040 | tf_op jit(solution)/shard_map/reduce_scatter | solution.py:90
  41.5 9.0 %collective-permute-start = (bf16[128,768]{1,0:T(8,128)(2,1)S(1)}, bf16[128,768]{1,0:T(8,128)(2,1)S(1)}, u32[]{:S(2)}, u32[]{:S(2)}) collective-permute-start(bf16[128,768]{1,0:T(8,128)(2,1)S(1)} %get-tuple-element.558), channel_id=1, source_target_pairs={{0,4},{4,8},{8,12},{12,0},{1,5},{5,9},{9,13},{13,1},{2,6},{6,10},{... | collective-permute-start | bytes 589832 | tf_op jit(solution)/shard_map/while/body/eval_jaxpr/ppermute | solution.py:12
  51.7 8.2 %collective-permute-start = (bf16[128,768]{1,0:T(8,128)(2,1)S(1)}, bf16[128,768]{1,0:T(8,128)(2,1)S(1)}, u32[]{:S(2)}, u32[]{:S(2)}) collective-permute-start(bf16[128,768]{1,0:T(8,128)(2,1)S(1)} %get-tuple-element.558), channel_id=1, source_target_pairs={{0,4},{4,8},{8,12},{12,0},{1,5},{5,9},{9,13},{13,1},{2,6},{6,10},{... | collective-permute-start | bytes 589832 | tf_op jit(solution)/shard_map/while/body/eval_jaxpr/ppermute | solution.py:12
  61.1 7.5 %collective-permute-start = (bf16[128,768]{1,0:T(8,128)(2,1)S(1)}, bf16[128,768]{1,0:T(8,128)(2,1)S(1)}, u32[]{:S(2)}, u32[]{:S(2)}) collective-permute-start(bf16[128,768]{1,0:T(8,128)(2,1)S(1)} %get-tuple-element.558), channel_id=1, source_target_pairs={{0,4},{4,8},{8,12},{12,0},{1,5},{5,9},{9,13},{13,1},{2,6},{6,10},{... | collective-permute-start | bytes 589832 | tf_op jit(solution)/shard_map/while/body/eval_jaxpr/ppermute | solution.py:12
  69.8 29.7 %copy-start.1 = (bf16[256,384]{1,0:T(8,128)(2,1)S(1)}, bf16[256,384]{1,0:T(8,128)(2,1)}, u32[]{:S(2)}) copy-start(bf16[256,384]{1,0:T(8,128)(2,1)} %param.6) | copy-start | bytes 589828
  71.0 89.8 %all-reduce.2.cloned.1.call-start = ((), (), s32[]{:S(2)}) async-start(), calls=%async_computation.4 | async-start | bytes 2359296 | tf_op jit(solution)/shard_map/psum | solution.py:103
Sparse Core Ops, SparseCore 0:
  10.8 20.1 reduce-scatter.2
  71.1 20.8 reduce-scatter.4
  101.1 59.6 all-reduce.1
where the time goes:
time: 170 us
  waiting for transfers between devices  114 us (67%)
  blocking collectives  15.7 us (9%)
  between operations  13.8 us (8%)
  other arithmetic  9.37 us (6%)
  matrix products  8.66 us (5%)
  local copies, waits for them, and re-layouts  6.9 us (4%)
  starting transfers between devices  1.78 us (1%)
    psum x1, waiting for transfers between devices, body(): head_grad = lax.psum(head_part, ('loop', 'rep'))  58.8 us
    reduce_scatter x1, waiting for transfers between devices, body(): lax.psum_scatter(grad_block.astype(jnp.bfloat16), ('enc', 'rep'), scatter...  20.9 us
    ppermute x3, waiting for transfers between devices, passed_along(): return lax.ppermute(value, axis, pairs)  17 us
    reduce_scatter x1, waiting for transfers between devices, body(): lax.psum_scatter(jnp.dot(rows, head_weight, preferred_element_type=jnp.fl...  16.8 us
    all_gather x1, blocking collectives, body(): block_feats = lax.all_gather(own_feats, ('enc', 'rep'), axis=0, tiled=True)  8.2 us
    all_gather x1, blocking collectives, body(): piece = lax.all_gather(own_grad, 'enc', axis=0, tiled=True)  7.51 us
    select_n x4, other arithmetic, tile(): piece_coef = jnp.where(piece_offsets < anchor_count, piece_coef, 0.0)  5.68 us
    unnamed x7, local copies, waits for them, and re-layouts  3.67 us
  transfers between devices with their start and end apart: 6, of which 6 were waited for; matrix products, arithmetic and copies ran while one was open for 6% of the time, Pallas kernels for 0%

commit v1 on v0

--- a/solution.py
+++ b/solution.py
@@ -100,7 +100,7 @@
         rows, piece, (((0,), (0,)), ((), ())), preferred_element_type=jnp.float32
     )
     embed_part, head_part = (embed_part, head_part)
-    head_grad = lax.psum(head_part, ("loop", "rep"))
+    head_grad = lax.psum(lax.psum(head_part, "rep"), "loop")
     return (embed_part.astype(jnp.bfloat16), head_grad)
 
 

time: 170 us -> 190 us (1.12)
  waiting for transfers between devices: 114 us -> 133 us
    psum x1 -> x2, waiting for transfers between devices: 58.8 us -> 78.3 us  [body(): head_grad = lax.psum(lax.psum(head_part, 'rep'), 'loop')]
  transfers between devices with their start and end apart: 6 -> 7, of which waited for: 6 -> 7; matrix products, arithmetic and copies ran while one was open for 6% -> 6% of each run, Pallas kernels for 0% -> 0%
where the time goes in v1:
time: 190 us
  waiting for transfers between devices  133 us (70%)
  blocking collectives  15.7 us (8%)
  between operations  13.8 us (7%)
  other arithmetic  9.37 us (5%)
  matrix products  8.66 us (5%)
  local copies, waits for them, and re-layouts  6.9 us (4%)
    psum x2, waiting for transfers between devices, body(): head_grad = lax.psum(lax.psum(head_part, 'rep'), 'loop')  78.3 us
    reduce_scatter x1, waiting for transfers between devices, body(): lax.psum_scatter(grad_block.astype(jnp.bfloat16), ('enc', 'rep'), scatter...  20.9 us
    ppermute x3, waiting for transfers between devices, passed_along(): return lax.ppermute(value, axis, pairs)  17 us
    reduce_scatter x1, waiting for transfers between devices, body(): lax.psum_scatter(jnp.dot(rows, head_weight, preferred_element_type=jnp.fl...  16.8 us
    all_gather x1, blocking collectives, body(): block_feats = lax.all_gather(own_feats, ('enc', 'rep'), axis=0, tiled=True)  8.2 us
    all_gather x1, blocking collectives, body(): piece = lax.all_gather(own_grad, 'enc', axis=0, tiled=True)  7.51 us
    select_n x4, other arithmetic, tile(): piece_coef = jnp.where(piece_offsets < anchor_count, piece_coef, 0.0)  5.68 us
  transfers between devices with their start and end apart: 7, of which 7 were waited for; matrix products, arithmetic and copies ran while one was open for 6% of the time, Pallas kernels for 0%

profile of v1, /device:TPU:0, one launch (start us, length us, event | category | flops | bytes accessed | tf_op | source)
XLA Modules:
  0.0 189.6 jit_solution(10322466684044067335)
XLA Ops:
  7.2 1.0 copy-done
  8.2 2.2 %fusion.40 = f32[256,768]{1,0:T(8,128)} fusion(bf16[256,384]{1,0:T(8,128)(2,1)} %param.6, bf16[384,768]{1,0:T(8,128)(2,1)S(1)} %copy-done), kind=kOutput, calls=%fused_computation.56 | convolution fusion | flops 150994944 | bytes 1572864 | tf_op jit(solution)/shard_map/dot_general | solution.py:31
  10.5 0.7 dynamic_slice.37
  11.2 0.8 dynamic_slice.39
  12.0 0.8 compare_select_fusion.1
  12.8 1.5 compare_select_fusion.2
  14.2 16.8 %reduce-scatter.3.cloned.1.call-done = f32[128,768]{1,0:T(8,128)} async-done(((f32[256,768]{1,0:T(8,128)}), f32[128,768]{1,0:T(8,128)}) %reduce-scatter.3.cloned.1.call-update) | async-done | bytes 393232 | tf_op jit(solution)/shard_map/reduce_scatter | solution.py:30
  31.0 1.1 multiply_reduce_fusion.1
  32.1 8.2 %all_gather.6 = bf16[512,768]{1,0:T(8,128)(2,1)S(1)} all-gather(bf16[128,768]{1,0:T(8,128)(2,1)S(1)} %get-tuple-element.541), channel_id=1, replica_groups=mesh['groups'=2,'loop'=4,'enc'=2,'rep'=2] {'enc','rep'}, dimensions={0}, use_global_device_ids=true | all-gather | bytes 983040 | tf_op jit(solution)/shard_map/all_gather | solution.py:36
  41.0 0.5 fusion.30
  41.5 28.3 %while.23 = (s32[]{:T(128)}, bf16[128,768]{1,0:T(8,128)(2,1)S(1)}, f32[512,768]{1,0:T(8,128)S(1)}, f32[512]{0:T(512)S(1)}, s32[]{:T(128)}, /*index=5*/s32[4]{0:T...) while((s32[]{:T(128)}, bf16[128,768]{1,0:T(8,128)(2,1)S(1)}, ...), condition=%wide.region_7.8_spmd.clone.clone, body=%wide.region_4.7_spmd.clone.clone.sunk | while | flops 203260192 | bytes 6246334 | solution.py:87
  41.5 1.5 collective-permute-start
  43.1 0.6 dynamic_slice.49
  43.6 1.4 compare_select_fusion.4
  45.1 5.5 %collective-permute-done = bf16[128,768]{1,0:T(8,128)(2,1)S(1)} collective-permute-done((bf16[128,768]{1,0:T(8,128)(2,1)S(1)}, bf16[128,768]{1,0:T(8,128)(2,1)S(1)}, u32[]{:S(2)}, u32[]{:S(2)}) %collective-permute-start) | collective-permute-done | bytes 196640 | tf_op jit(solution)/shard_map/while/body/eval_jaxpr/ppermute | solution.py:12
  51.1 0.6 convolution_add_fusion.2
  51.8 0.6 dynamic_slice.49
  52.4 1.4 compare_select_fusion.4
  53.8 6.1 %collective-permute-done = bf16[128,768]{1,0:T(8,128)(2,1)S(1)} collective-permute-done((bf16[128,768]{1,0:T(8,128)(2,1)S(1)}, bf16[128,768]{1,0:T(8,128)(2,1)S(1)}, u32[]{:S(2)}, u32[]{:S(2)}) %collective-permute-start) | collective-permute-done | bytes 196640 | tf_op jit(solution)/shard_map/while/body/eval_jaxpr/ppermute | solution.py:12
  60.5 0.6 convolution_add_fusion.2
  61.2 0.6 dynamic_slice.49
  61.8 1.4 compare_select_fusion.4
  63.2 5.4 %collective-permute-done = bf16[128,768]{1,0:T(8,128)(2,1)S(1)} collective-permute-done((bf16[128,768]{1,0:T(8,128)(2,1)S(1)}, bf16[128,768]{1,0:T(8,128)(2,1)S(1)}, u32[]{:S(2)}, u32[]{:S(2)}) %collective-permute-start) | collective-permute-done | bytes 196640 | tf_op jit(solution)/shard_map/while/body/eval_jaxpr/ppermute | solution.py:12
  69.2 0.6 convolution_add_fusion.2
  69.8 1.1 fusion.21
  71.1 20.9 %reduce-scatter.5.cloned.1.call-done = bf16[128,768]{1,0:T(8,128)(2,1)} async-done(((bf16[512,768]{1,0:T(8,128)(2,1)}), bf16[128,768]{1,0:T(8,128)(2,1)}) %reduce-scatter.5.cloned.1.call-update) | async-done | bytes 196624 | tf_op jit(solution)/shard_map/reduce_scatter | solution.py:90
  92.0 7.5 %all_gather.7 = bf16[256,768]{1,0:T(8,128)(2,1)S(1)} all-gather(bf16[128,768]{1,0:T(8,128)(2,1)} %reduce-scatter.5.cloned.1.call-done), channel_id=1, replica_groups=mesh['groups'=2,'loop'=4,'enc'=2,'rep'=2] {'enc'}, dimensions={0}, use_global_device_ids=true | all-gather | bytes 589824 | tf_op jit(solution)/shard_map/all_gather | solution.py:93
  99.5 1.4 convolution_bitcast_fusion
  101.0 19.9 %all-reduce.3.cloned.1.call-done = f32[384,768]{0,1:T(8,128)} async-done(((f32[384,768]{0,1:T(8,128)}), f32[384,768]{0,1:T(8,128)}) %all-reduce.3.cloned.1.call-update) | async-done | bytes 1179664 | tf_op jit(solution)/shard_map/psum | solution.py:103
  121.0 1.1 convolution_convert_fusion
  122.0 58.4 %all-reduce.5.cloned.1.call-done = f32[384,768]{0,1:T(8,128)} async-done(((f32[384,768]{0,1:T(8,128)}), f32[384,768]{0,1:T(8,128)}) %all-reduce.5.cloned.1.call-update) | async-done | bytes 1179664 | tf_op jit(solution)/shard_map/psum | solution.py:103
  180.4 2.7 %copy.9 = f32[384,768]{1,0:T(8,128)} copy(f32[384,768]{0,1:T(8,128)} %all-reduce.5.cloned.1.call-done) | data formatting | bytes 2359296
  (32 shorter events, 2.9 us)
Async XLA Ops:
  7.2 1.1 copy-start
  7.2 3.3 %copy-start.2 = (s32[4]{0:T(128)S(1)}, s32[4]{0:T(128)}, u32[]{:S(2)}) copy-start(s32[4]{0:T(128)} %param.9) | copy-start | bytes 52
  7.2 23.8 %reduce-scatter.3.cloned.1.call-start = ((), (), s32[]{:S(2)}) async-start(), calls=%async_computation.2 | async-start | bytes 1179648 | tf_op jit(solution)/shard_map/reduce_scatter | solution.py:30
  10.4 81.6 %reduce-scatter.5.cloned.1.call-start = ((), (), s32[]{:S(2)}) async-start(), calls=%async_computation.3 | async-start | bytes 983040 | tf_op jit(solution)/shard_map/reduce_scatter | solution.py:90
  41.5 9.0 %collective-permute-start = (bf16[128,768]{1,0:T(8,128)(2,1)S(1)}, bf16[128,768]{1,0:T(8,128)(2,1)S(1)}, u32[]{:S(2)}, u32[]{:S(2)}) collective-permute-start(bf16[128,768]{1,0:T(8,128)(2,1)S(1)} %get-tuple-element.558), channel_id=1, source_target_pairs={{0,4},{4,8},{8,12},{12,0},{1,5},{5,9},{9,13},{13,1},{2,6},{6,10},{... | collective-permute-start | bytes 589832 | tf_op jit(solution)/shard_map/while/body/eval_jaxpr/ppermute | solution.py:12
  51.7 8.2 %collective-permute-start = (bf16[128,768]{1,0:T(8,128)(2,1)S(1)}, bf16[128,768]{1,0:T(8,128)(2,1)S(1)}, u32[]{:S(2)}, u32[]{:S(2)}) collective-permute-start(bf16[128,768]{1,0:T(8,128)(2,1)S(1)} %get-tuple-element.558), channel_id=1, source_target_pairs={{0,4},{4,8},{8,12},{12,0},{1,5},{5,9},{9,13},{13,1},{2,6},{6,10},{... | collective-permute-start | bytes 589832 | tf_op jit(solution)/shard_map/while/body/eval_jaxpr/ppermute | solution.py:12
  61.1 7.5 %collective-permute-start = (bf16[128,768]{1,0:T(8,128)(2,1)S(1)}, bf16[128,768]{1,0:T(8,128)(2,1)S(1)}, u32[]{:S(2)}, u32[]{:S(2)}) collective-permute-start(bf16[128,768]{1,0:T(8,128)(2,1)S(1)} %get-tuple-element.558), channel_id=1, source_target_pairs={{0,4},{4,8},{8,12},{12,0},{1,5},{5,9},{9,13},{13,1},{2,6},{6,10},{... | collective-permute-start | bytes 589832 | tf_op jit(solution)/shard_map/while/body/eval_jaxpr/ppermute | solution.py:12
  69.8 29.7 %copy-start.1 = (bf16[256,384]{1,0:T(8,128)(2,1)S(1)}, bf16[256,384]{1,0:T(8,128)(2,1)}, u32[]{:S(2)}) copy-start(bf16[256,384]{1,0:T(8,128)(2,1)} %param.6) | copy-start | bytes 589828
  71.0 49.9 %all-reduce.3.cloned.1.call-start = ((), (), s32[]{:S(2)}) async-start(), calls=%async_computation.4 | async-start | bytes 2359296 | tf_op jit(solution)/shard_map/psum | solution.py:103
  100.9 79.5 %all-reduce.5.cloned.1.call-start = ((), (), s32[]{:S(2)}) async-start(), calls=%async_computation.5 | async-start | bytes 2359296 | tf_op jit(solution)/shard_map/psum | solution.py:103
Sparse Core Ops, SparseCore 0:
  10.8 20.1 reduce-scatter.2
  71.1 20.8 reduce-scatter.4
  101.1 19.8 all-reduce.2
  123.3 57.0 all-reduce.4
